TPU v7x, 32 devices: a whole 2x2x4 slice. The times are simulated.
32 devices in a mesh: depth: 16 (over z, y, core), filt: 2 (over x).
Axes of the slice: x: 2, y: 2, z: 4, core: 2. Of those that a mesh axis runs over, the one named last changes fastest.
Arguments:
- volume: bfloat16 [64, 64, 4096], P('filt', 'depth'), may hold values from -6 to 6
- w_three: bfloat16 [1728, 128], P(None, 'filt'), may hold values from -0.15625 to 0.15625
- w_four: bfloat16 [3456, 256], P(None, 'filt'), may hold values from -0.109375 to 0.109375
- cotangent: bfloat16 [256, 16, 256], P('filt', 'depth'), may hold values from -384 to 384
Outputs:
- x_grad: float32 [64, 64, 4096], P('filt', 'depth')
- w3_grad: float32 [1728, 128], P(None, 'filt')
- w4_grad: float32 [3456, 256], P(None, 'filt')
All inputs are finite; a program needn't handle non-finite values.
Results may differ from a plain program's by a relative error of at most 0.014.
Values may be sent and summed in bfloat16 or wider, within the bound.
No kernel may reach another device: no remote copies, remote signals or barrier semaphores. Data moves between devices by JAX's collectives and lax.ppermute only.
A program may use at most 192 MiB of HBM per device.

v0:
```python
import math

import jax
import jax.numpy as jnp
from jax import lax
from jax.sharding import PartitionSpec as P

HH = 32
WW = 128


def padded_2(block, sides, width):
    for axis, dim in sides:
        count = lax.axis_size(axis)
        forward = [(i, i + 1) for i in range(count - 1)]
        backward = [(target, source) for source, target in forward]
        low = lax.ppermute(
            lax.slice_in_dim(block, block.shape[dim] - width, None, axis=dim), axis, forward
        )
        high = lax.ppermute(lax.slice_in_dim(block, 0, width, axis=dim), axis, backward)
        block = jnp.concatenate([low, block, high], axis=dim)
    return block


def conv_slab(framed, kernel):
    return lax.conv_general_dilated(
        framed[None],
        kernel,
        (1, 1, 1),
        [(0, 0), (1, 1), (1, 1)],
        dimension_numbers=("NCDHW", "OIDHW", "NCDHW"),
        preferred_element_type=jnp.float32,
    )[0]


def forward_kernel(matrix, inputs, outputs):
    return matrix.reshape(3, 3, 3, inputs, outputs).transpose(4, 3, 0, 1, 2)


def backward_kernel(matrix, inputs, outputs):
    return matrix.reshape(3, 3, 3, inputs, outputs)[::-1, ::-1, ::-1].transpose(3, 4, 0, 1, 2)


def average_pool(field):
    chans, deep, tall, broad = field.shape
    return field.reshape(chans, deep // 2, 2, tall // 2, 2, broad // 2, 2).mean(axis=(2, 4, 6))


def spread_back(field):
    return jnp.repeat(jnp.repeat(jnp.repeat(field, 2, 1), 2, 2), 2, 3) / 8.0


def silu_slope(value):
    sigma = jax.nn.sigmoid(value)
    return sigma * (1.0 + value * (1.0 - sigma))


def kernel_tile(framed, grads):
    chans = framed.shape[0]
    planes = grads.shape[1]
    tall = grads.shape[2]
    broad = grads.shape[3]
    padded = jnp.pad(framed, ((0, 0), (0, 0), (0, 0), (1, 1)))
    blocks = []
    for depth_step in range(3):
        for height_step in range(3):
            for width_step in range(3):
                window = padded[
                    :,
                    depth_step : depth_step + planes,
                    height_step : height_step + tall,
                    width_step : width_step + broad,
                ]
                blocks.append(
                    jnp.einsum("cdhw,odhw->co", window, grads, preferred_element_type=jnp.float32)
                )
    return jnp.stack(blocks).reshape(27 * chans, grads.shape[0])


def kernel_grad(framed, grads):
    padded = jnp.pad(framed, ((0, 0), (0, 0), (1, 1), (0, 0)))
    return kernel_tile(padded, grads)


def channel_plan(volume, w_three, w_four, cotangent):
    own_in, planes, cells = volume.shape
    c_in = w_three.shape[0] // 27
    mid_own = w_three.shape[1]
    c_mid = w_four.shape[0] // 27
    out_own = w_four.shape[1]
    tall = HH
    broad = WW
    all_planes = planes * lax.axis_size("depth")
    channels = lax.all_gather(volume, "filt", axis=0, tiled=True)
    framed = padded_2(channels, (("depth", 1),), 1)
    grid_three = framed.reshape(c_in, planes + 2, tall, broad)
    pre_three = conv_slab(grid_three, forward_kernel(w_three, c_in, mid_own))
    pooled = average_pool(jax.nn.silu(pre_three)).astype(jnp.bfloat16)
    half_planes = planes // 2
    pooled_flat = pooled.reshape(mid_own, half_planes, tall // 2 * (broad // 2))
    pooled_all = lax.all_gather(pooled_flat, "filt", axis=0, tiled=True)
    pooled_framed = padded_2(pooled_all, (("depth", 1),), 1)
    grid_four = pooled_framed.reshape(c_mid, half_planes + 2, tall // 2, broad // 2)
    pre_four = conv_slab(grid_four, forward_kernel(w_four, c_mid, out_own))
    upper = cotangent.astype(jnp.float32).reshape(out_own, planes // 4, tall // 4, broad // 4)
    grad_four = (spread_back(upper) * silu_slope(pre_four)).astype(jnp.bfloat16)
    coarse_kernel = kernel_grad(grid_four, grad_four)
    coarse_kernel = lax.psum(coarse_kernel, "depth")
    grad_four_framed = padded_2(grad_four.reshape(out_own, half_planes, -1), (("depth", 1),), 1)
    coarse_grid = grad_four_framed.reshape(out_own, half_planes + 2, tall // 2, broad // 2)
    coarse_back = backward_kernel(w_four, c_mid, out_own)
    sliced = coarse_back
    pooled_grad = lax.psum_scatter(
        conv_slab(coarse_grid, sliced)
        .reshape(lax.axis_size("filt") * mid_own, half_planes, -1)
        .astype(jnp.bfloat16),
        "filt",
        scatter_dimension=0,
        tiled=True,
    ).astype(jnp.float32)
    pooled_grad = pooled_grad.reshape(mid_own, half_planes, tall // 2, broad // 2)
    grad_three = (spread_back(pooled_grad) * silu_slope(pre_three)).astype(jnp.bfloat16)
    fine_kernel = kernel_grad(grid_three, grad_three)
    fine_kernel = lax.psum(fine_kernel, "depth")
    grad_three_framed = padded_2(grad_three.reshape(mid_own, planes, -1), (("depth", 1),), 1)
    fine_grid = grad_three_framed.reshape(mid_own, planes + 2, tall, broad)
    fine_back = backward_kernel(w_three, c_in, mid_own)
    sliced = fine_back
    x_grad = lax.psum_scatter(
        conv_slab(fine_grid, sliced)
        .reshape(lax.axis_size("filt") * own_in, planes, -1)
        .astype(jnp.bfloat16),
        "filt",
        scatter_dimension=0,
        tiled=True,
    ).astype(jnp.float32)
    scale_four = 1.0 / math.sqrt(all_planes * tall * broad / 8.0)
    scale_three = 1.0 / math.sqrt(all_planes * tall * broad * 1.0)
    return (x_grad, fine_kernel * scale_three, coarse_kernel * scale_four)


def body(volume, w_three, w_four, cotangent):
    return channel_plan(volume, w_three, w_four, cotangent)


def solution(mesh):
    return jax.shard_map(
        body,
        mesh=mesh,
        in_specs=(
            P("filt", "depth", None),
            P(None, "filt"),
            P(None, "filt"),
            P("filt", "depth", None),
        ),
        out_specs=(P("filt", "depth", None), P(None, "filt"), P(None, "filt")),
        check_vma=False,
    )
```

profile of v0, /device:TPU:0, one launch (start us, length us, event | category | flops | bytes accessed | tf_op | source)
XLA Modules:
  0.0 529.5 jit_solution(11492941788564465801)
XLA Ops:
  8.0 37.4 %all-gather.2.cloned.1.call-done = bf16[64,4,4096]{2,1,0:T(4,128)(2,1)} async-done(((bf16[32,4,4096]{2,1,0:T(4,128)(2,1)}), bf16[64,4,4096]{2,1,0:T(4,128)(2,1)}) %all-gather.2.cloned.1.call-update) | async-done | bytes 2097168 | tf_op jit(solution)/shard_map/all_gather | solution.py:94
  45.4 4.7 fusion.271
  53.3 4.1 collective-permute-start
  63.8 4.7 pad_maximum_fusion
  68.5 7.6 %reshape.223 = bf16[64,6,32,1,128]{4,2,1,0,3:T(8,128)(2,1)} reshape(bf16[64,6,4096]{2,1,0:T(8,128)(2,1)} %pad_maximum_fusion) | data formatting | bytes 6291456 | tf_op jit(solution)/shard_map/broadcast_in_dim;reshape | solution.py:27
  76.1 12.2 %copy.589 = bf16[64,6,32,1,128]{0,2,4,1,3:T(8,128)(2,1)} copy(bf16[64,6,32,1,128]{4,2,1,0,3:T(8,128)(2,1)} %reshape.223) | data formatting | bytes 6291456
  88.3 4.1 pad.20.clone
  97.8 21.5 %add_multiply_fusion = (f32[4,32,8,17,64]{4,2,3,1,0:T(8,128)}, f32[4,32,8,17,64]{4,2,3,1,0:T(8,128)S(1)}) fusion(bf16[3,3,3,64,64]{4,3,2,1,0:T(8,128)(2,1)S(1)} %bitcast.650, bf16[64,6,32,1,7,2]{0,4,5,2,1,3:T(8,128)(2,1)S(1)} %slice.284, bf16[64,6,32,1,8,17]{0,4,5,2,1,3:T(8,128)(2,1)} %copy-done.7, pred[8,17]{0,1:T(8,128)(4,1)S(1)} %copy-done.15), kind=kOutput, calls=%fused_computation.22 | convolution fusion | flops 3790274560 | bytes 12820616 | tf_op jit(solution)/shard_map/conv_general_dilated | solution.py:26
  119.3 5.0 copy.428
  124.3 11.6 %fusion.269 = (f32[4,32,1,128,64]{4,1,3,0,2:T(8,128)}, f32[1,64,4,32,128]{1,3,4,2,0:T(8,128)}) fusion(f32[4,32,1,136,64]{4,1,3,0,2:T(8,128)} %bitcast.623), kind=kLoop, calls=%fused_computation.356 | loop fusion | bytes 12582912 | tf_op jit(solution)/shard_map/conv_general_dilated | solution.py:26
  135.9 8.2 %copy.430 = f32[1,64,4,32,128]{1,4,3,2,0:T(8,128)S(1)} copy(f32[1,64,4,32,128]{1,3,4,2,0:T(8,128)} %get-tuple-element.18) | data formatting | bytes 8388608 | tf_op jit(solution)/shard_map/conv_general_dilated | solution.py:26
  144.2 11.4 %fusion.4 = f32[64,2,16,64]{0,3,2,1:T(8,128)S(1)} fusion(f32[64,2,2,16,2,64,2]{0,6,5,4,3,2,1:T(2,128)S(1)} %bitcast.626), kind=kLoop, calls=%fused_computation.27 | loop fusion | flops 5111808 | bytes 4718592 | tf_op jit(solution)/shard_map/reduce_sum | solution.py:46
  156.0 7.0 %all_gather.7 = bf16[128,2,1024]{2,1,0:T(2,128)(2,1)S(1)} all-gather(bf16[64,2,1024]{2,1,0:T(2,128)(2,1)S(1)} %copy.431), channel_id=1, replica_groups=mesh['depth'=16,'filt'=2] {'filt'}, dimensions={0}, use_global_device_ids=true | all-gather | bytes 786432 | tf_op jit(solution)/shard_map/all_gather | solution.py:101
  164.9 7.4 %collective-permute-start.2 = (bf16[128,1,1024]{0,2,1:T(8,128)(2,1)S(1)}, bf16[128,1,1024]{0,2,1:T(8,128)(2,1)}, u32[]{:S(2)}, u32[]{:S(2)}) collective-permute-start(bf16[128,1,1024]{0,2,1:T(8,128)(2,1)S(1)} %get-tuple-element.25), channel_id=1, source_target_pairs={{0,2},{2,4},{4,6},{6,8},{8,10},{10,12},{12,14},{14,16},{16,18},{18... | collective-permute-start | bytes 786440 | tf_op jit(solution)/shard_map/ppermute | solution.py:17
  174.2 7.6 %reshape.225 = bf16[64,6,32,128]{3,2,1,0:T(8,128)(2,1)} reshape(bf16[64,6,4096]{2,1,0:T(8,128)(2,1)} %pad_maximum_fusion) | data formatting | bytes 6291456 | tf_op jit(solution)/shard_map/reshape | solution.py:96
  181.8 8.7 %copy.587 = f32[4,32,1,128,64]{3,1,0,4,2:T(8,128)} copy(f32[4,32,1,128,64]{4,1,3,0,2:T(8,128)} %get-tuple-element.17) | data formatting | bytes 8388608
  190.6 5.5 %reshape.224 = f32[64,4,4096]{2,1,0:T(4,128)} reshape(f32[1,64,4,32,128]{4,3,2,1,0:T(8,128)} %bitcast.620) | data formatting | bytes 8388608 | tf_op jit(solution)/shard_map/squeeze | solution.py:26
  196.1 8.7 %copy.454 = f32[4,32,8,17,64]{4,1,3,2,0:T(8,128)} copy(f32[4,32,8,17,64]{4,2,3,1,0:T(8,128)} %get-tuple-element.29) | data formatting | bytes 8912896 | tf_op jit(solution)/shard_map/mul | solution.py:55
  204.8 3.7 copy.463
  211.8 4.7 add_multiply_fusion.1
  219.1 5.9 %collective-permute-start.4 = (bf16[128,1,1024]{0,2,1:T(8,128)(2,1)S(1)}, bf16[128,1,1024]{0,2,1:T(8,128)(2,1)S(1)}, u32[]{:S(2)}, u32[]{:S(2)}) collective-permute-start(bf16[128,1,1024]{0,2,1:T(8,128)(2,1)S(1)} %get-tuple-element.23), channel_id=1, source_target_pairs={{0,2},{2,4},{4,6},{6,8},{8,10},{10,12},{12,14},{14,16},{16,18},{18... | collective-permute-start | bytes 786440 | tf_op jit(solution)/shard_map/ppermute | solution.py:17
  236.4 4.3 fusion.72
  245.3 27.8 %all-reduce.9.cloned.1.call-done = bf16[128,2,1024]{2,1,0:T(2,128)(2,1)} async-done(((bf16[128,2,1024]{2,1,0:T(2,128)(2,1)}), bf16[128,2,1024]{2,1,0:T(2,128)(2,1)}) %all-reduce.9.cloned.1.call-update) | async-done | bytes 524304
  280.3 4.5 broadcast_in_dim.28.clone
  284.8 6.8 %copy.453 = f32[64,4,4096]{2,0,1:T(8,128)} copy(f32[64,4,4096]{0,2,1:T(8,128)} %bitcast.625) | data formatting | bytes 8388608 | tf_op jit(solution)/shard_map/div | solution.py:50
  291.6 6.6 %multiply_convert_fusion = bf16[64,4,4096]{2,0,1:T(8,128)(2,1)S(1)} fusion(f32[64,4,4096]{2,0,1:T(8,128)} %copy.453, f32[64,4,4096]{2,1,0:T(4,128)} %reshape.224), kind=kLoop, calls=%fused_computation.53 | loop fusion | flops 9437184 | bytes 10485760 | tf_op jit(solution)/shard_map/convert_element_type | solution.py:122
  299.5 3.1 collective-permute-start.6
  302.6 4.5 broadcast_in_dim.28
  307.2 9.1 %copy.464 = f32[64,4,32,128]{3,2,1,0:T(8,128)} copy(f32[64,4,32,128]{0,2,3,1:T(8,128)} %bitcast.618) | data formatting | bytes 8388608 | tf_op jit(solution)/shard_map/div | solution.py:50
  316.3 5.2 fusion.25
  323.3 3.1 fusion.143
  329.7 3.3 fusion.146
  336.3 4.7 fusion.142
  344.3 3.0 fusion.141
  350.6 3.2 fusion.145
  357.1 5.0 fusion.140
  365.4 3.1 fusion.139
  372.0 3.1 fusion.144
  378.4 5.1 fusion.138
  386.2 9.9 %fusion.3 = bf16[1,64,4,32,128]{1,3,4,2,0:T(8,128)(2,1)} fusion(f32[1,64,4,32,128]{1,3,4,2,0:T(8,128)} %bitcast.619, f32[4,32,1,136,64]{4,1,3,0,2:T(8,128)} %bitcast.624), kind=kLoop, calls=%fused_computation.26 | loop fusion | flops 2097152 | bytes 10485760 | tf_op jit(solution)/shard_map/convert_element_type | solution.py:122
  399.7 3.8 maximum_bitcast_fusion
  407.8 32.0 %select_convert_fusion = bf16[4,32,8,17,64]{4,2,3,1,0:T(8,128)(2,1)S(1)} fusion(pred[8,17]{0,1:T(8,128)(4,1)S(1)} %copy-done.16, bf16[3,3,3,64,64]{4,3,2,1,0:T(8,128)(2,1)S(1)} %bitcast.651, bf16[64,6,32,1,7,2]{0,4,5,2,1,3:T(8,128)(2,1)S(1)} %slice.298, bf16[64,6,32,1,8,17]{0,4,5,2,1,3:T(8,128)(2,1)S(1)} %copy.458), kind=kOutput, calls=%fused_computation.21 | convolution fusion | flops 3783589888 | bytes 6135944 | tf_op jit(solution)/shard_map/conv_general_dilated | solution.py:26
  440.7 2.7 slice_bitcast_fusion.1
  443.4 7.7 %copy.461 = bf16[1,64,4,32,128]{4,3,1,2,0:T(8,128)(2,1)S(1)} copy(bf16[1,64,4,32,128]{1,3,4,2,0:T(8,128)(2,1)} %slice_bitcast_fusion.1) | data formatting | bytes 4194304 | tf_op jit(solution)/shard_map/convert_element_type | solution.py:132
  453.5 32.1 %all-reduce.11.cloned.1.call-done = (f32[1728,64]{0,1:T(8,128)}, f32[3456,128]{1,0:T(8,128)}) async-done(((f32[1728,64]{0,1:T(8,128)}, f32[3456,128]{1,0:T(8,128)}), (f32[1728,64]{0,1:T(8,128)}, f32[3456,128]{1,0:T(8,128)})) %all-reduce.11.cloned.1.call-update) | async-done | bytes 2211856 | tf_op jit(solution)/shard_map/psum | solution.py:124
  487.4 2.9 broadcast_multiply_fusion
  490.3 29.1 %reduce-scatter.2.cloned.1.call-done = bf16[32,4,4096]{2,0,1:T(8,128)(2,1)} async-done(((bf16[64,4,4096]{2,0,1:T(8,128)(2,1)}), bf16[32,4,4096]{2,0,1:T(8,128)(2,1)}) %reduce-scatter.2.cloned.1.call-update) | async-done | bytes 1048592 | tf_op jit(solution)/shard_map/reduce_scatter | solution.py:129
  519.4 3.4 copy.524
  (160 shorter events, 93.1 us)
Async XLA Ops:
  7.2 204.5 %copy-start = (bf16[3456,128]{1,0:T(8,128)(2,1)S(1)}, bf16[3456,128]{1,0:T(8,128)(2,1)}, u32[]{:S(2)}) copy-start(bf16[3456,128]{1,0:T(8,128)(2,1)} %param.6) | copy-start | bytes 2654212
  7.2 38.2 %all-gather.2.cloned.1.call-start = ((), (), s32[]{:S(2)}) async-start(), calls=%async_computation.1 | async-start | bytes 3145728 | tf_op jit(solution)/shard_map/all_gather | solution.py:94
  7.9 265.2 %all-reduce.9.cloned.1.call-start = ((), (), s32[]{:S(2)}) async-start(), calls=%async_computation.3 | async-start | bytes 1048576
  50.7 8.7 %collective-permute-start.1 = (bf16[64,1,4096]{2,0,1:T(8,128)(2,1)S(1)}, bf16[64,1,4096]{2,0,1:T(8,128)(2,1)}, u32[]{:S(2)}, u32[]{:S(2)}) collective-permute-start(bf16[64,1,4096]{2,0,1:T(8,128)(2,1)S(1)} %copy.420), channel_id=1, source_target_pairs={{2,0},{4,2},{6,4},{8,6},{10,8},{12,10},{14,12},{16,14},{18,16},{20... | collective-permute-start | bytes 1572872 | tf_op jit(solution)/shard_map/ppermute | solution.py:20
  53.3 10.5 %copy-start.6 = (bf16[64,4,4096]{2,1,0:T(4,128)(2,1)S(1)}, bf16[64,4,4096]{2,1,0:T(4,128)(2,1)}, u32[]{:S(2)}) copy-start(bf16[64,4,4096]{2,1,0:T(4,128)(2,1)} %all-gather.2.cloned.1.call-done) | copy-start | bytes 6291460
  53.3 8.2 %collective-permute-start = (bf16[64,1,4096]{2,0,1:T(8,128)(2,1)}, bf16[64,1,4096]{2,0,1:T(8,128)(2,1)}, u32[]{:S(2)}, u32[]{:S(2)}) collective-permute-start(bf16[64,1,4096]{2,0,1:T(8,128)(2,1)} %copy.419), channel_id=1, source_target_pairs={{0,2},{2,4},{4,6},{6,8},{8,10},{10,12},{12,14},{14,16},{16,18},{18... | collective-permute-start | bytes 1572872 | tf_op jit(solution)/shard_map/ppermute | solution.py:17
  92.4 5.4 %copy-start.10 = (bf16[1728,64]{1,0:T(8,128)(2,1)S(1)}, bf16[1728,64]{1,0:T(8,128)(2,1)}, u32[]{:S(2)}) copy-start(bf16[1728,64]{1,0:T(8,128)(2,1)} %copy.586) | copy-start | bytes 663556
  92.4 5.4 %copy-start.15 = (pred[8,17]{0,1:T(8,128)(4,1)S(1)}, pred[8,17]{0,1:T(8,128)(4,1)}, u32[]{:S(2)}) copy-start(pred[8,17]{0,1:T(8,128)(4,1)} %constant.47) | copy-start | bytes 412
  95.0 2.8 copy-start.7
  155.7 16.6 %copy-start.13 = (bf16[128,1,256]{2,0,1:T(8,128)(2,1)S(1)}, bf16[128,1,256]{2,0,1:T(8,128)(2,1)}, u32[]{:S(2)}) copy-start(bf16[128,1,256]{2,0,1:T(8,128)(2,1)} %param.7) | copy-start | bytes 196612
  163.0 10.0 %copy-start.14 = (u32[32]{0:T(128)S(1)}, u32[32]{0:T(128)}, u32[]{:S(2)}) copy-start(u32[32]{0:T(128)} %constant.53) | copy-start | bytes 388
  163.6 44.9 %collective-permute-start.3 = (bf16[128,1,1024]{0,2,1:T(8,128)(2,1)S(1)}, bf16[128,1,1024]{0,2,1:T(8,128)(2,1)S(1)}, u32[]{:S(2)}, u32[]{:S(2)}) collective-permute-start(bf16[128,1,1024]{0,2,1:T(8,128)(2,1)S(1)} %get-tuple-element.26), channel_id=1, source_target_pairs={{2,0},{4,2},{6,4},{8,6},{10,8},{12,10},{14,12},{16,14},{18,16},{20... | collective-permute-start | bytes 786440 | tf_op jit(solution)/shard_map/ppermute | solution.py:20
  164.9 44.3 %collective-permute-start.2 = (bf16[128,1,1024]{0,2,1:T(8,128)(2,1)S(1)}, bf16[128,1,1024]{0,2,1:T(8,128)(2,1)}, u32[]{:S(2)}, u32[]{:S(2)}) collective-permute-start(bf16[128,1,1024]{0,2,1:T(8,128)(2,1)S(1)} %get-tuple-element.25), channel_id=1, source_target_pairs={{0,2},{2,4},{4,6},{6,8},{8,10},{10,12},{12,14},{14,16},{16,18},{18... | collective-permute-start | bytes 786440 | tf_op jit(solution)/shard_map/ppermute | solution.py:17
  196.1 8.7 %copy-start.4 = (bf16[64,6,32,128]{3,2,1,0:T(8,128)(2,1)S(1)}, bf16[64,6,32,128]{3,2,1,0:T(8,128)(2,1)}, u32[]{:S(2)}) copy-start(bf16[64,6,32,128]{3,2,1,0:T(8,128)(2,1)} %reshape.225) | copy-start | bytes 9437188
  208.5 0.7 copy-start.12
  211.1 0.7 copy-start.17
  217.6 17.7 %collective-permute-start.5 = (bf16[128,1,1024]{0,2,1:T(8,128)(2,1)S(1)}, bf16[128,1,1024]{0,2,1:T(8,128)(2,1)S(1)}, u32[]{:S(2)}, u32[]{:S(2)}) collective-permute-start(bf16[128,1,1024]{0,2,1:T(8,128)(2,1)S(1)} %get-tuple-element.24), channel_id=1, source_target_pairs={{2,0},{4,2},{6,4},{8,6},{10,8},{12,10},{14,12},{16,14},{18,16},{20... | collective-permute-start | bytes 786440 | tf_op jit(solution)/shard_map/ppermute | solution.py:20
  219.1 16.4 %collective-permute-start.4 = (bf16[128,1,1024]{0,2,1:T(8,128)(2,1)S(1)}, bf16[128,1,1024]{0,2,1:T(8,128)(2,1)S(1)}, u32[]{:S(2)}, u32[]{:S(2)}) collective-permute-start(bf16[128,1,1024]{0,2,1:T(8,128)(2,1)S(1)} %get-tuple-element.23), channel_id=1, source_target_pairs={{0,2},{2,4},{4,6},{6,8},{8,10},{10,12},{12,14},{14,16},{16,18},{18... | collective-permute-start | bytes 786440 | tf_op jit(solution)/shard_map/ppermute | solution.py:17
  234.0 1.2 copy-start.9
  242.1 243.4 %all-reduce.11.cloned.1.call-start = ((), (), s32[]{:S(2)}) async-start(), calls=%async_computation.4 | async-start | bytes 4456448 | tf_op jit(solution)/shard_map/psum | solution.py:124
  277.8 2.4 copy-start.2
  291.6 11.0 %copy-start.3 = (f32[64,4,16,2,64]{0,3,2,4,1:T(2,128)S(1)}, f32[64,4,16,2,64]{0,3,2,4,1:T(2,128)}, u32[]{:S(2)}) copy-start(f32[64,4,16,2,64]{0,3,2,4,1:T(2,128)} %copy-done.2) | copy-start | bytes 6291460
  298.2 97.9 %collective-permute-start.7 = (bf16[64,1,4096]{2,0,1:T(8,128)(2,1)S(1)}, bf16[64,1,4096]{2,0,1:T(8,128)(2,1)S(1)}, u32[]{:S(2)}, u32[]{:S(2)}) collective-permute-start(bf16[64,1,4096]{2,0,1:T(8,128)(2,1)S(1)} %get-tuple-element.20), channel_id=1, source_target_pairs={{2,0},{4,2},{6,4},{8,6},{10,8},{12,10},{14,12},{16,14},{18,16},{20... | collective-permute-start | bytes 1572872 | tf_op jit(solution)/shard_map/ppermute | solution.py:20
  299.5 98.4 %collective-permute-start.6 = (bf16[64,1,4096]{2,0,1:T(8,128)(2,1)S(1)}, bf16[64,1,4096]{2,0,1:T(8,128)(2,1)S(1)}, u32[]{:S(2)}, u32[]{:S(2)}) collective-permute-start(bf16[64,1,4096]{2,0,1:T(8,128)(2,1)S(1)} %get-tuple-element.19), channel_id=1, source_target_pairs={{0,2},{2,4},{4,6},{6,8},{8,10},{10,12},{12,14},{14,16},{16,18},{18... | collective-permute-start | bytes 1572872 | tf_op jit(solution)/shard_map/ppermute | solution.py:17
  316.3 5.2 copy-start.8
  321.4 1.9 copy-start.5
  386.2 133.2 %reduce-scatter.2.cloned.1.call-start = ((), (), s32[]{:S(2)}) async-start(), calls=%async_computation.2 | async-start | bytes 3145728 | tf_op jit(solution)/shard_map/reduce_scatter | solution.py:129
  404.9 2.8 copy-start.11
  404.9 2.8 copy-start.16
  487.4 35.4 %copy-start.1 = (bf16[3456,128]{1,0:T(8,128)(2,1)S(1)}, bf16[3456,128]{1,0:T(8,128)(2,1)}, u32[]{:S(2)}) copy-start(bf16[3456,128]{1,0:T(8,128)(2,1)} %param.6) | copy-start | bytes 2654212
Sparse Core Ops, SparseCore 0:
  9.6 35.7 all-gather.1
  242.3 30.7 all-reduce.8
  386.3 99.1 all-reduce.10
  488.3 31.0 reduce-scatter.1
where the time goes:
time: 533 us; the launch traced here: 529 us
  local copies, waits for them, and re-layouts  168 us (32%)
  matrix products  137 us (26%)
  waiting for transfers between devices  127 us (24%)
  other arithmetic  48.6 us (9%)
  starting transfers between devices  26 us (5%)
  between operations  15.7 us (3%)
  blocking collectives  7.05 us (1%)
    dot_general x54, matrix products, kernel_tile(): jnp.einsum('cdhw,odhw->co', window, grads, preferred_element_type=jnp.flo...  74.6 us
    conv_general_dilated x4, matrix products, conv_slab(): lax.conv_general_dilated(framed[None], kernel, (1, 1, 1), [(0, 0), (1, 1)...  62.5 us
    all_gather x1, waiting for transfers between devices, channel_plan(): channels = lax.all_gather(volume, 'filt', axis=0, tiled=True)  37.4 us
    unnamed x46, local copies, waits for them, and re-layouts  34.3 us
    psum x1, waiting for transfers between devices, channel_plan(): fine_kernel = lax.psum(fine_kernel, 'depth')  32.1 us
    conv_general_dilated x14, local copies, waits for them, and re-layouts, conv_slab(): lax.conv_general_dilated(framed[None], kernel, (1, 1, 1), [(0, 0), (1, 1)...  31.8 us
    reduce_scatter x1, waiting for transfers between devices, channel_plan(): lax.psum_scatter(conv_slab(fine_grid, sliced).reshape(lax.axis_size('filt...  29.1 us
    unnamed x5, waiting for transfers between devices  28.5 us
  transfers between devices with their start and end apart: 12, of which 4 were waited for; matrix products, arithmetic and copies ran while one was open for 39% of the time, Pallas kernels for 0%

commit v1 on v0

v1 whole, which is shorter than its diff:
```python
import functools
import math

import jax
import jax.numpy as jnp
import numpy as np
from jax import lax
from jax.experimental import pallas as pl
from jax.experimental.pallas import tpu as pltpu
from jax.sharding import PartitionSpec as P

HH = 32
WW = 128
LANES = 128
BF = jnp.bfloat16
F32 = jnp.float32
VMEM_LIMIT = 56 * 2**20
TILES = HH // 4


def nn(a, b):
    return jnp.dot(a, b, preferred_element_type=F32)


def nt(a, b):
    return lax.dot_general(a, b, (((1,), (1,)), ((), ())), preferred_element_type=F32)


def call(body, outs, name, scratch=(), scalars=0, inputs=0):
    specs = [pl.BlockSpec(memory_space=pltpu.SMEM)] * scalars
    specs += [pl.BlockSpec(memory_space=pltpu.VMEM)] * inputs
    return pl.pallas_call(
        body,
        out_shape=[jax.ShapeDtypeStruct(shape, dtype) for shape, dtype in outs],
        in_specs=specs,
        out_specs=[pl.BlockSpec(memory_space=pltpu.VMEM)] * len(outs),
        scratch_shapes=list(scratch),
        compiler_params=pltpu.CompilerParams(vmem_limit_bytes=VMEM_LIMIT),
        name=name,
    )


def sigmoid(value):
    return 0.5 * jnp.tanh(0.5 * value) + 0.5


def shifted(block, width):
    wide = block.astype(F32)
    lane = lax.broadcasted_iota(jnp.int32, wide.shape, 1) % width
    before = jnp.where(lane == 0, 0.0, pltpu.roll(wide, 1, axis=1)).astype(BF)
    after = jnp.where(lane == width - 1, 0.0, pltpu.roll(wide, LANES - 1, axis=1)).astype(BF)
    return before, after


def fine_rows(source, windows, plane, offset, chans, group, first, count):
    def row(step, _):
        block = source(step)
        before, after = shifted(block, WW)
        lanes = pl.ds(pl.multiple_of((step - first + 1) * LANES, LANES), LANES)
        for shift, value in enumerate((before, block, after)):
            windows[plane, pl.ds(pl.multiple_of(shift * group + offset, 32), chans), lanes] = value
        return 0

    lower = max(first - 1, 0)
    upper = min(first + count + 1, HH)
    zero = jnp.zeros((chans, LANES), BF)
    for shift in range(3):
        rows = pl.ds(pl.multiple_of(shift * group + offset, 32), chans)
        if first == 0:
            windows[plane, rows, 0:LANES] = zero
        if first + count == HH:
            windows[plane, rows, (count + 1) * LANES : (count + 2) * LANES] = zero
    lax.fori_loop(lower, upper, row, 0, unroll=2)


def row_of(ref):
    def source(step):
        return ref[:, pl.ds(pl.multiple_of(step * LANES, LANES), LANES)]

    return source


def coarse_rows(source, windows, plane, offset, chans, group):
    half = LANES // 2
    lane = lax.broadcasted_iota(jnp.int32, (chans, LANES), 1)

    def put(shift, tile, value):
        rows = pl.ds(pl.multiple_of(shift * group + offset, 32), chans)
        windows[plane, rows, tile * LANES : (tile + 1) * LANES] = value

    for tile in range(TILES):
        block = source(tile)
        before, after = shifted(block, half)
        for shift, value in enumerate((before, block, after)):
            put(shift, tile + 1, value)
            if tile == 0 or tile == TILES - 1:
                turned = pltpu.roll(value.astype(F32), half, axis=1)
                if tile == TILES - 1:
                    put(shift, 0, jnp.where(lane < half, 0.0, turned).astype(BF))
                else:
                    put(shift, TILES + 1, jnp.where(lane < half, turned, 0.0).astype(BF))


def tile_of(ref):
    def source(tile):
        return ref[:, tile * LANES : (tile + 1) * LANES]

    return source


def window_planes(refs, own):
    own_ref, low, high, edge, middle, peer_low, peer_high = refs
    planes = own_ref.shape[0]
    out = [(0, low, True), (planes + 1, high, True)]
    out += [(d + 1, own_ref.at[d], True) for d in range(planes)]
    out += [(0, peer_low, False), (planes + 1, peer_high, False)]
    out += [(1, edge.at[0], False), (planes, edge.at[1], False)]
    out += [(d + 2, middle.at[d], False) for d in range(planes - 2)]
    return out


def forward_fine_kernel(filt, own, low, high, edge, middle, plow, phigh, weights, pool, pooled, slope, windows):
    chans = own.shape[1]
    planes = own.shape[0]
    mine = pl.multiple_of(filt[0] * chans, 32)
    theirs = pl.multiple_of((1 - filt[0]) * chans, 32)
    for plane, ref, is_own in window_planes((own, low, high, edge, middle, plow, phigh), True):
        fine_rows(row_of(ref), windows, plane, mine if is_own else theirs, chans, 2 * chans, 0, HH)
    outs = weights.shape[1] // 3
    span = 2 * LANES

    def chunk(j, _):
        tops = (j * 2, HH // 2 + j * 2)
        acts = []
        for d in range(planes):
            acts.append([None, None])
        for side, top in enumerate(tops):
            totals = [None] * planes
            for p in range(planes + 2):
                value = None
                for kh in range(3):
                    lanes = pl.ds(pl.multiple_of((top + kh) * LANES, LANES), span)
                    part = nn(weights[kh], windows[p, :, lanes])
                    value = part if value is None else value + part
                for kd in range(3):
                    d = p - kd
                    if 0 <= d < planes:
                        piece = value[kd * outs : (kd + 1) * outs]
                        totals[d] = piece if totals[d] is None else totals[d] + piece
            for d in range(planes):
                pre = totals[d]
                sigma = sigmoid(pre)
                act = pre * sigma
                slope[d, :, pl.ds(pl.multiple_of(top * LANES, LANES), span)] = (
                    sigma + act * (1.0 - sigma)
                ).astype(BF)
                acts[d][side] = act[:, :LANES] + act[:, LANES:]
        for d in range(0, planes, 2):
            both = jnp.concatenate(
                [acts[d][0] + acts[d + 1][0], acts[d][1] + acts[d + 1][1]], axis=1
            )
            coarse = both.astype(BF)
            rest = (both - coarse.astype(F32)).astype(BF)
            mean = nn(coarse, pool[...]) + nn(rest, pool[...])
            pooled[d // 2, :, pl.ds(pl.multiple_of(j * LANES, LANES), LANES)] = mean.astype(BF)
        return 0

    lax.fori_loop(0, TILES, chunk, 0)


def forward_coarse_kernel(filt, own, low, high, peer, plow, phigh, weights, cot, spread, grads, windows):
    planes, chans, cells = own.shape
    mine = pl.multiple_of(filt[0] * chans, 32)
    theirs = pl.multiple_of((1 - filt[0]) * chans, 32)
    sides = ((mine, low, own, high), (theirs, plow, peer, phigh))
    for offset, below, middle, above in sides:
        refs = [below] + [middle.at[d] for d in range(planes)] + [above]
        for plane, ref in enumerate(refs):
            coarse_rows(tile_of(ref), windows, plane, offset, chans, 2 * chans)
    upper = nn(cot[...], spread[...])
    span = cells // 2
    for d in range(planes):
        for start in range(0, cells, span):
            pre = None
            for kd in range(3):
                for kh in range(3):
                    begin = start + kh * LANES
                    part = nn(weights[kd * 3 + kh], windows[d + kd, :, begin : begin + span])
                    pre = part if pre is None else pre + part
            sigma = sigmoid(pre)
            slope = sigma * (1.0 + pre * (1.0 - sigma))
            grads[d, :, start : start + span] = (upper[:, start : start + span] * slope).astype(BF)


def kernel_grad_coarse_kernel(windows, grads, out, total):
    deep, group, _ = windows.shape
    planes = deep - 2
    outs = grads.shape[0] // planes
    cells = grads.shape[1]
    seen = set()
    for p in range(deep):
        first, last = max(p - 2, 0), min(p, planes - 1)
        for kh in range(3):
            value = nt(
                windows[p, :, kh * LANES : kh * LANES + cells],
                grads[first * outs : (last + 1) * outs, :],
            )
            for d in range(first, last + 1):
                index = (p - d) * 3 + kh
                rows = slice(index * group, (index + 1) * group)
                part = value[:, (d - first) * outs : (d - first + 1) * outs]
                total[rows, :] = total[rows, :] + part if index in seen else part
                seen.add(index)
    out[...] = total[...].astype(out.dtype)


def backward_coarse_kernel(grads, low, high, weights, own, peer, windows):
    planes, chans, cells = grads.shape
    refs = [low] + [grads.at[d] for d in range(planes)] + [high]
    for plane, ref in enumerate(refs):
        coarse_rows(tile_of(ref), windows, plane, 0, chans, chans)
    half = weights.shape[1] // 2
    span = cells // 2
    for d in range(planes):
        for start in range(0, cells, span):
            value = None
            for kd in range(3):
                for kh in range(3):
                    begin = start + kh * LANES
                    part = nn(weights[kd * 3 + kh], windows[d + kd, :, begin : begin + span])
                    value = part if value is None else value + part
            own[d, :, start : start + span] = value[:half]
            peer[d, :, start : start + span] = value[half:].astype(BF)


def grad_fine_kernel(own, peer, slope, unpool, grads):
    planes = own.shape[0]
    for d in range(planes):
        for j in range(TILES):
            lanes = slice(j * LANES, (j + 1) * LANES)
            block = (own[d, :, lanes] + peer[d, :, lanes].astype(F32)).astype(BF)
            wide = nn(block, unpool[...])
            for side in range(2):
                part = wide[:, side * LANES : (side + 1) * LANES]
                for a in range(2):
                    for row in (side * HH // 2 + 2 * j, side * HH // 2 + 2 * j + 1):
                        cells = slice(row * LANES, (row + 1) * LANES)
                        grads[2 * d + a, :, cells] = (
                            part * slope[2 * d + a, :, cells].astype(F32)
                        ).astype(BF)


def kernel_grad_fine_kernel(filt, own, low, high, edge, middle, plow, phigh, grads, out, windows, total):
    planes, chans, cells = own.shape
    mine = pl.multiple_of(filt[0] * chans, 32)
    theirs = pl.multiple_of((1 - filt[0]) * chans, 32)
    for plane, ref, is_own in window_planes((own, low, high, edge, middle, plow, phigh), True):
        fine_rows(row_of(ref), windows, plane, mine if is_own else theirs, chans, 2 * chans, 0, HH)
    group = windows.shape[1]
    outs = grads.shape[0] // planes
    seen = set()
    for p in range(planes + 2):
        first, last = max(p - 2, 0), min(p, planes - 1)
        for kh in range(3):
            value = nt(
                windows[p, :, kh * LANES : kh * LANES + cells],
                grads[first * outs : (last + 1) * outs, :],
            )
            for d in range(first, last + 1):
                index = (p - d) * 3 + kh
                rows = slice(index * group, (index + 1) * group)
                part = value[:, (d - first) * outs : (d - first + 1) * outs]
                total[rows, :] = total[rows, :] + part if index in seen else part
                seen.add(index)
    out[...] = total[...].astype(out.dtype)


def backward_fine_kernel(first, count, grads, low, high, weights, own, peer, windows):
    planes, chans, _ = grads.shape
    refs = [low] + [grads.at[d] for d in range(planes)] + [high]
    for plane, ref in enumerate(refs):
        fine_rows(row_of(ref), windows, plane, 0, chans, chans, first, count)
    outs = weights.shape[1] // 3
    half = outs // 2
    span = 2 * LANES

    def chunk(j, _):
        totals = [None] * planes
        for p in range(planes + 2):
            value = None
            for kh in range(3):
                lanes = pl.ds(pl.multiple_of((2 * j + kh) * LANES, LANES), span)
                part = nn(weights[kh], windows[p, :, lanes])
                value = part if value is None else value + part
            for kd in range(3):
                d = p - kd
                if 0 <= d < planes:
                    piece = value[kd * outs : (kd + 1) * outs]
                    totals[d] = piece if totals[d] is None else totals[d] + piece
        cells = pl.ds(pl.multiple_of(j * span, span), span)
        for d in range(planes):
            own[d, :, cells] = totals[d][:half]
            peer[d, :, cells] = totals[d][half:].astype(BF)
        return 0

    lax.fori_loop(0, count // 2, chunk, 0)


def to_next(value):
    count = lax.axis_size("depth")
    return lax.ppermute(value, "depth", [(i, i + 1) for i in range(count - 1)])


def to_previous(value):
    count = lax.axis_size("depth")
    return lax.ppermute(value, "depth", [(i + 1, i) for i in range(count - 1)])


def swap(value):
    return lax.ppermute(value, "filt", [(0, 1), (1, 0)])


def sum_over_depth(value):
    count = lax.axis_size("depth")
    place = lax.axis_index("depth")
    bits = [1 << k for k in range(count.bit_length() - 1)]
    rows = value.shape[0]
    value = jnp.pad(value, ((0, -rows % (8 * count)), (0, 0)))
    for bit in bits:
        half = value.shape[0] // 2
        upper = (place & bit) != 0
        keep = jnp.where(upper, value[half:], value[:half])
        send = jnp.where(upper, value[:half], value[half:])
        other = lax.ppermute(send, "depth", [(i, i ^ bit) for i in range(count)])
        value = (keep.astype(F32) + other.astype(F32)).astype(value.dtype)
    for bit in reversed(bits):
        upper = (place & bit) != 0
        other = lax.ppermute(value, "depth", [(i, i ^ bit) for i in range(count)])
        value = jnp.concatenate(
            [jnp.where(upper, other, value), jnp.where(upper, value, other)], axis=0
        )
    return value[:rows]


def pool_matrix():
    lane = np.arange(2 * LANES)
    column = np.where(lane < LANES, lane // 2, LANES // 2 + (lane - LANES) // 2)
    return (np.arange(LANES)[None] == column[:, None]) * np.float32(0.125)


def spread_matrix(tall, broad):
    lane = np.arange(4 * tall * broad)
    tile, half, w = lane // LANES, lane % LANES // (2 * broad), lane % (2 * broad)
    row = tile + half * TILES
    cell = row // 2 * broad + w // 2
    return (np.arange(tall * broad)[:, None] == cell[None]) * np.float32(0.125)


def body(volume, w_three, w_four, cotangent):
    own_in, planes, cells = volume.shape
    mid = w_three.shape[1]
    c_mid = w_four.shape[0] // 27
    outs = w_four.shape[1]
    half_planes = planes // 2
    coarse = cells // 4
    filt = lax.axis_index("filt")
    which = filt.astype(jnp.int32).reshape(1)

    own = volume.transpose(1, 0, 2)
    edge = swap(jnp.stack([own[0], own[planes - 1]]))
    middle = swap(own[1 : planes - 1])
    low, high = to_next(own[planes - 1]), to_previous(own[0])
    plow, phigh = to_next(edge[1]), to_previous(edge[0])

    fine = w_three.reshape(3, 3, 3, 2 * own_in, mid)
    fine_forward = fine.transpose(1, 0, 4, 2, 3).reshape(3, 3 * mid, 6 * own_in)
    turned = fine[::-1, ::-1, ::-1].reshape(3, 3, 3, 2, own_in, mid)
    turned = jnp.where(filt == 0, turned, turned[:, :, :, ::-1])
    fine_backward = turned.transpose(1, 0, 3, 4, 2, 5).reshape(3, 6 * own_in, 3 * mid)
    wide = w_four.reshape(3, 3, 3, c_mid, outs)
    wide_forward = wide.transpose(0, 1, 4, 2, 3).reshape(9, outs, 3 * c_mid)
    turned = wide[::-1, ::-1, ::-1].reshape(3, 3, 3, 2, mid, outs)
    turned = jnp.where(filt == 0, turned, turned[:, :, :, ::-1])
    wide_backward = turned.transpose(0, 1, 3, 4, 2, 5).reshape(9, c_mid, 3 * outs)
    pool = jnp.asarray(pool_matrix(), BF)
    unpool = jnp.asarray(pool_matrix().T, BF)
    spread = jnp.asarray(spread_matrix(HH // 4, WW // 4), BF)

    fine_windows = pltpu.VMEM((planes + 2, 6 * own_in, (HH + 2) * LANES), BF)
    pooled, slope = call(
        forward_fine_kernel,
        [((half_planes, mid, coarse), BF), ((planes, mid, cells), BF)],
        "forward_fine",
        [fine_windows],
        scalars=1,
        inputs=9,
    )(which, own, low, high, edge, middle, plow, phigh, fine_forward, pool)

    pooled_peer = swap(pooled)
    pool_low, pool_high = to_next(pooled[half_planes - 1]), to_previous(pooled[0])
    ppool_low, ppool_high = to_next(pooled_peer[half_planes - 1]), to_previous(pooled_peer[0])
    coarse_lanes = (TILES + 2) * LANES
    grad_four, coarse_windows = call(
        forward_coarse_kernel,
        [
            ((half_planes, outs, coarse), BF),
            ((half_planes + 2, 3 * c_mid, coarse_lanes), BF),
        ],
        "forward_coarse",
        scalars=1,
        inputs=9,
    )(
        which,
        pooled,
        pool_low,
        pool_high,
        pooled_peer,
        ppool_low,
        ppool_high,
        wide_forward,
        cotangent.reshape(outs, -1),
        spread,
    )

    four_low, four_high = to_next(grad_four[half_planes - 1]), to_previous(grad_four[0])
    (coarse_kernel,) = call(
        kernel_grad_coarse_kernel,
        [((27 * c_mid, outs), BF)],
        "kernel_grad_coarse",
        [pltpu.VMEM((27 * c_mid, outs), F32)],
        inputs=2,
    )(coarse_windows, grad_four.reshape(half_planes * outs, coarse))
    own_back, peer_back = call(
        backward_coarse_kernel,
        [((half_planes, mid, coarse), F32), ((half_planes, mid, coarse), BF)],
        "backward_coarse",
        [pltpu.VMEM((half_planes + 2, 3 * outs, coarse_lanes), BF)],
        inputs=4,
    )(grad_four, four_low, four_high, wide_backward)
    peer_back = swap(peer_back)
    coarse_sum = sum_over_depth(coarse_kernel)

    (grad_three,) = call(
        grad_fine_kernel, [((planes, mid, cells), BF)], "grad_fine", inputs=4
    )(own_back, peer_back, slope, unpool)
    three_low, three_high = to_next(grad_three[planes - 1]), to_previous(grad_three[0])
    (fine_kernel,) = call(
        kernel_grad_fine_kernel,
        [((54 * own_in, mid), BF)],
        "kernel_grad_fine",
        [fine_windows, pltpu.VMEM((54 * own_in, mid), F32)],
        scalars=1,
        inputs=8,
    )(which, own, low, high, edge, middle, plow, phigh, grad_three.reshape(planes * mid, cells))
    fine_sum = sum_over_depth(fine_kernel.reshape(27 * own_in, 2 * mid)).reshape(54 * own_in, mid)

    parts = 2
    count = HH // parts
    owns, peers = [], []
    for part in range(parts):
        mine, theirs = call(
            functools.partial(backward_fine_kernel, part * count, count),
            [((planes, own_in, count * WW), F32), ((planes, own_in, count * WW), BF)],
            f"backward_fine_{part}",
            [pltpu.VMEM((planes + 2, 3 * mid, (count + 2) * LANES), BF)],
            inputs=4,
        )(grad_three, three_low, three_high, fine_backward)
        owns.append(mine)
        peers.append(swap(theirs))
    x_grad = jnp.concatenate([a + b.astype(F32) for a, b in zip(owns, peers)], axis=2)
    x_grad = x_grad.transpose(1, 0, 2)

    all_cells = planes * lax.axis_size("depth") * cells
    scale_four = 1.0 / math.sqrt(all_cells / 8.0)
    scale_three = 1.0 / math.sqrt(all_cells * 1.0)
    return (x_grad, fine_sum.astype(F32) * scale_three, coarse_sum.astype(F32) * scale_four)


def solution(mesh):
    return jax.shard_map(
        body,
        mesh=mesh,
        in_specs=(
            P("filt", "depth", None),
            P(None, "filt"),
            P(None, "filt"),
            P("filt", "depth", None),
        ),
        out_specs=(P("filt", "depth", None), P(None, "filt"), P(None, "filt")),
        check_vma=False,
    )
```

time: 533 us -> 245 us (0.46)
  local copies, waits for them, and re-layouts: 168 us -> 29.4 us
  matrix products: 137 us -> 0 us
  Pallas kernels: 0 us -> 103 us
  waiting for transfers between devices: 127 us -> 54 us
  other arithmetic: 48.6 us -> 3.69 us
  starting transfers between devices: 26 us -> 53 us
  between operations: 15.7 us -> 1.34 us
  blocking collectives: 7.05 us -> 0 us
    pallas_call x0 -> x8, Pallas kernels: none -> 103 us  [the longest x1 29.1 us: body(): call(forward_fine_kernel, [((half_planes, mid, coarse), BF), ((planes, mi...]
    dot_general x54 -> x0, matrix products: 74.6 us -> none  [kernel_tile(): jnp.einsum('cdhw,odhw->co', window, grads, preferred_element_type=jnp.flo...]
    conv_general_dilated x4 -> x0, matrix products: 62.5 us -> none  [conv_slab(): lax.conv_general_dilated(framed[None], kernel, (1, 1, 1), [(0, 0), (1, 1)...]
    ppermute x8 -> x34, waiting for transfers between devices: 0.02 us -> 54 us  [the longest x6 27.8 us: swap(): return lax.ppermute(value, 'filt', [(0, 1), (1, 0)])]
    all_gather x1 -> x0, waiting for transfers between devices: 37.4 us -> none  [channel_plan(): channels = lax.all_gather(volume, 'filt', axis=0, tiled=True)]
    psum x1 -> x0, waiting for transfers between devices: 32.1 us -> none  [channel_plan(): fine_kernel = lax.psum(fine_kernel, 'depth')]
    conv_general_dilated x14 -> x0, local copies, waits for them, and re-layouts: 31.8 us -> none  [conv_slab(): lax.conv_general_dilated(framed[None], kernel, (1, 1, 1), [(0, 0), (1, 1)...]
    reduce_scatter x1 -> x0, waiting for transfers between devices: 29.1 us -> none  [channel_plan(): lax.psum_scatter(conv_slab(fine_grid, sliced).reshape(lax.axis_size('filt...]
  transfers between devices with their start and end apart: 12 -> 34, of which waited for: 4 -> 13; matrix products, arithmetic and copies ran while one was open for 39% -> 9% of each run, Pallas kernels for 0% -> 25%
where the time goes in v1:
time: 245 us; the launch traced here: 244 us
  Pallas kernels  103 us (42%)
  waiting for transfers between devices  54 us (22%)
  starting transfers between devices  53 us (22%)
  local copies, waits for them, and re-layouts  29.4 us (12%)
  other arithmetic  3.69 us (2%)
    pallas_call x1, Pallas kernels, body(): call(forward_fine_kernel, [((half_planes, mid, coarse), BF), ((planes, mi...  29.1 us
    ppermute x6, waiting for transfers between devices, swap(): return lax.ppermute(value, 'filt', [(0, 1), (1, 0)])  27.8 us
    pallas_call x1, Pallas kernels, body(): call(kernel_grad_fine_kernel, [((54 * own_in, mid), BF)], 'kernel_grad_fi...  26.8 us
    pallas_call x2, Pallas kernels, body(): call(functools.partial(backward_fine_kernel, part * count, count), [((pla...  25.7 us
    ppermute x8, starting transfers between devices, sum_over_depth(): other = lax.ppermute(send, 'depth', [(i, i ^ bit) for i in range(count)])  18 us
    ppermute x6, starting transfers between devices, to_next(): return lax.ppermute(value, 'depth', [(i, i + 1) for i in range(count - 1)])  15.1 us
    ppermute x8, waiting for transfers between devices, sum_over_depth(): other = lax.ppermute(send, 'depth', [(i, i ^ bit) for i in range(count)])  13.5 us
    ppermute x8, waiting for transfers between devices, sum_over_depth(): other = lax.ppermute(value, 'depth', [(i, i ^ bit) for i in range(count)])  12.7 us
  transfers between devices with their start and end apart: 34, of which 13 were waited for; matrix products, arithmetic and copies ran while one was open for 9% of the time, Pallas kernels for 25%

profile of v1, /device:TPU:0, one launch (start us, length us, event | category | flops | bytes accessed | tf_op | source)
XLA Modules:
  0.0 244.2 jit_solution(2247393813922506758)
XLA Ops:
  0.6 1.8 copy.35
  3.5 3.0 %collective-permute-start.2 = (bf16[2,32,4096]{2,1,0:T(8,128)(2,1)S(1)}, bf16[2,32,4096]{2,1,0:T(8,128)(2,1)S(1)}, u32[]{:S(2)}, u32[]{:S(2)}) collective-permute-start(bf16[2,32,4096]{2,1,0:T(8,128)(2,1)S(1)} %pad_maximum_fusion), channel_id=1, source_target_pairs={{0,1},{1,0},{2,3},{3,2},{4,5},{5,4},{6,7},{7,6},{8,9},{9,8},{10,11... | collective-permute-start | bytes 1572872 | tf_op jit(solution)/shard_map/ppermute | solution.py:320
  6.5 1.5 collective-permute-start
  8.0 1.3 collective-permute-start.1
  10.4 8.8 %collective-permute-done.2.edge = bf16[2,32,4096]{2,1,0:T(8,128)(2,1)S(1)} collective-permute-done((bf16[2,32,4096]{2,1,0:T(8,128)(2,1)S(1)}, bf16[2,32,4096]{2,1,0:T(8,128)(2,1)S(1)}, u32[]{:S(2)}, u32[]{:S(2)}) %collective-permute-start.2) | collective-permute-done | bytes 524320 | tf_op jit(solution)/shard_map/ppermute | solution.py:320
  20.2 1.3 collective-permute-start.4
  21.5 1.3 collective-permute-start.5
  24.5 5.2 %collective-permute-done.3.middle = bf16[2,32,4096]{2,1,0:T(8,128)(2,1)S(1)} collective-permute-done((bf16[2,32,4096]{2,1,0:T(8,128)(2,1)}, bf16[2,32,4096]{2,1,0:T(8,128)(2,1)S(1)}, u32[]{:S(2)}, u32[]{:S(2)}) %collective-permute-start.3) | collective-permute-done | bytes 524320 | tf_op jit(solution)/shard_map/ppermute | solution.py:320
  30.7 29.1 %forward_fine.1 = (bf16[2,64,1024]{2,1,0:T(8,128)(2,1)}, bf16[4,64,4096]{2,1,0:T(8,128)(2,1)}) custom-call(s32[1]{0:T(128)} %bitcast.filt, bf16[4,32,4096]{2,1,0:T(8,128)(2,1)} %bitcast.50, bf16[32,4096]{1,0:T(8,128)(2,1)} %copy-done.8, bf16[32,4096]{1,0:T(8,128)(2,1)} %copy-done.9, bf16[2,32,4096]{2,1,0:T(8,128)(2,1)} %copy-done.3, ...), custom_call_target="tpu_custom_call" | custom-call | tf_op jit(solution)/shard_map/forward_fine/pallas_call | solution.py:390
  59.8 1.7 collective-permute-start.8
  62.5 3.6 %collective-permute-start.6 = (bf16[64,1024]{1,0:T(8,128)(2,1)S(1)}, bf16[64,1024]{1,0:T(8,128)(2,1)S(1)}, u32[]{:S(2)}, u32[]{:S(2)}) collective-permute-start(bf16[64,1024]{1,0:T(8,128)(2,1)S(1)} %get-tuple-element.49), channel_id=1, source_target_pairs={{0,2},{2,4},{4,6},{6,8},{8,10},{10,12},{12,14},{14,16},{16,18},{18... | collective-permute-start | bytes 393224 | tf_op jit(solution)/shard_map/ppermute | solution.py:311
  66.1 1.3 collective-permute-start.7
  68.6 1.3 collective-permute-start.10
  69.8 3.7 %collective-permute-start.9 = (bf16[64,1024]{1,0:T(8,128)(2,1)S(1)}, bf16[64,1024]{1,0:T(8,128)(2,1)S(1)}, u32[]{:S(2)}, u32[]{:S(2)}) collective-permute-start(bf16[64,1024]{1,0:T(8,128)(2,1)S(1)} %get-tuple-element.47), channel_id=1, source_target_pairs={{0,2},{2,4},{4,6},{6,8},{8,10},{10,12},{12,14},{14,16},{16,18},{18... | collective-permute-start | bytes 393224 | tf_op jit(solution)/shard_map/ppermute | solution.py:311
  73.5 1.7 rev.14
  75.3 1.7 copy.27.weights
  78.6 6.3 %forward_coarse.1 = (bf16[2,128,1024]{2,1,0:T(8,128)(2,1)}, bf16[4,384,1280]{2,1,0:T(8,128)(2,1)}) custom-call(s32[1]{0:T(128)} %bitcast.filt, bf16[2,64,1024]{2,1,0:T(8,128)(2,1)} %get-tuple-element.13.own, bf16[64,1024]{1,0:T(8,128)(2,1)} %copy-done.19, bf16[64,1024]{1,0:T(8,128)(2,1)} %copy-done.20, bf16[2,64,1024]{2,1,0:T(8,128)(2,1)} %copy-done.14, ...), custom_call_target="tpu_custom_call" | custom-call | tf_op jit(solution)/shard_map/forward_coarse/pallas_call | solution.py:403
  86.0 3.7 %collective-permute-start.11 = (bf16[128,1024]{1,0:T(8,128)(2,1)S(1)}, bf16[128,1024]{1,0:T(8,128)(2,1)S(1)}, u32[]{:S(2)}, u32[]{:S(2)}) collective-permute-start(bf16[128,1024]{1,0:T(8,128)(2,1)S(1)} %get-tuple-element.41), channel_id=1, source_target_pairs={{0,2},{2,4},{4,6},{6,8},{8,10},{10,12},{12,14},{14,16},{16,18},{18... | collective-permute-start | bytes 786440 | tf_op jit(solution)/shard_map/ppermute | solution.py:311
  89.7 1.5 collective-permute-start.12
  91.8 2.0 reshape.57.weights
  94.7 5.8 %kernel_grad_coarse.1 = bf16[3456,128]{1,0:T(8,128)(2,1)} custom-call(bf16[4,384,1280]{2,1,0:T(8,128)(2,1)} %get-tuple-element.22.windows, bf16[256,1024]{1,0:T(8,128)(2,1)} %bitcast.53), custom_call_target="tpu_custom_call" | custom-call | tf_op jit(solution)/shard_map/kernel_grad_coarse/pallas_call | solution.py:426
  101.9 5.4 %backward_coarse.1 = (f32[2,64,1024]{2,1,0:T(8,128)}, bf16[2,64,1024]{2,1,0:T(8,128)(2,1)}) custom-call(bf16[2,128,1024]{2,1,0:T(8,128)(2,1)} %get-tuple-element.14.grads, bf16[128,1024]{1,0:T(8,128)(2,1)} %copy-done.16, bf16[128,1024]{1,0:T(8,128)(2,1)} %copy-done.17, bf16[9,128,384]{2,1,0:T(8,128)(2,1)} %reshape.57.weights), custom_call_target="tpu_custom_call" | custom-call | tf_op jit(solution)/shard_map/backward_coarse/pallas_call | solution.py:433
  107.2 1.7 collective-permute-start.13
  109.0 1.3 collective-permute-start.26
  111.9 3.9 %collective-permute-done.13.peer = bf16[2,64,1024]{2,1,0:T(8,128)(2,1)S(1)} collective-permute-done((bf16[2,64,1024]{2,1,0:T(8,128)(2,1)}, bf16[2,64,1024]{2,1,0:T(8,128)(2,1)S(1)}, u32[]{:S(2)}, u32[]{:S(2)}) %collective-permute-start.13) | collective-permute-done | bytes 262176 | tf_op jit(solution)/shard_map/ppermute | solution.py:320
  116.5 3.7 %grad_fine.1.grads = bf16[4,64,4096]{2,1,0:T(8,128)(2,1)} custom-call(f32[2,64,1024]{2,1,0:T(8,128)} %get-tuple-element.15.own, bf16[2,64,1024]{2,1,0:T(8,128)(2,1)} %copy-done.15, bf16[4,64,4096]{2,1,0:T(8,128)(2,1)} %get-tuple-element.17.slope, bf16[128,256]{1,0:T(8,128)(2,1)} %constant.31.clone.unpool), custom_call_target="tpu_custom_call" | custom-call | tf_op jit(solution)/shard_map/grad_fine/pallas_call | solution.py:443
  120.3 26.8 %kernel_grad_fine.1 = bf16[1728,64]{1,0:T(8,128)(2,1)} custom-call(s32[1]{0:T(128)} %bitcast.filt, bf16[4,32,4096]{2,1,0:T(8,128)(2,1)} %bitcast.51, bf16[32,4096]{1,0:T(8,128)(2,1)} %copy-done.8, bf16[32,4096]{1,0:T(8,128)(2,1)} %copy-done.9, bf16[2,32,4096]{2,1,0:T(8,128)(2,1)} %copy-done.3, bf16[2,32,4096]{2,1,0:T(8,128)(2,1)} %copy-done.5, ...), custom_call_target="tpu_custom_call" | custom-call | tf_op jit(solution)/shard_map/kernel_grad_fine/pallas_call | solution.py:447
  151.2 4.1 %collective-permute-start.19 = (bf16[224,128]{1,0:T(8,128)(2,1)S(1)}, bf16[224,128]{1,0:T(8,128)(2,1)S(1)}, u32[]{:S(2)}, u32[]{:S(2)}) collective-permute-start(bf16[224,128]{1,0:T(8,128)(2,1)S(1)} %broadcast_select_fusion.14), channel_id=1, source_target_pairs={{0,4},{2,6},{4,0},{6,2},{8,12},{10,14},{12,8},{14,10},{16,20},{18,... | collective-permute-start | bytes 172040 | tf_op jit(solution)/shard_map/ppermute | solution.py:334
  155.4 2.2 collective-permute-done.19
  157.7 1.7 collective-permute-start.20
  159.4 1.3 collective-permute-start.14
  160.7 1.3 collective-permute-start.15
  162.1 7.0 %collective-permute-start.21 = (bf16[56,128]{1,0:T(8,128)(2,1)S(1)}, bf16[56,128]{1,0:T(8,128)(2,1)S(1)}, u32[]{:S(2)}, u32[]{:S(2)}) collective-permute-start(bf16[56,128]{1,0:T(8,128)(2,1)S(1)} %broadcast_select_fusion.23), channel_id=1, source_target_pairs={{0,16},{2,18},{4,20},{6,22},{8,24},{10,26},{12,28},{14,30},{16,0},... | collective-permute-start | bytes 43016 | tf_op jit(solution)/shard_map/ppermute | solution.py:334
  169.2 7.4 %collective-permute-done.21 = bf16[56,128]{1,0:T(8,128)(2,1)S(1)} collective-permute-done((bf16[56,128]{1,0:T(8,128)(2,1)S(1)}, bf16[56,128]{1,0:T(8,128)(2,1)S(1)}, u32[]{:S(2)}, u32[]{:S(2)}) %collective-permute-start.21) | collective-permute-done | bytes 14368 | tf_op jit(solution)/shard_map/ppermute | solution.py:334
  176.8 1.4 collective-permute-start.28
  178.2 3.3 %collective-permute-done.22 = bf16[56,128]{1,0:T(8,128)(2,1)S(1)} collective-permute-done((bf16[56,128]{1,0:T(8,128)(2,1)S(1)}, bf16[56,128]{1,0:T(8,128)(2,1)S(1)}, u32[]{:S(2)}, u32[]{:S(2)}) %collective-permute-start.22) | collective-permute-done | bytes 14368 | tf_op jit(solution)/shard_map/ppermute | solution.py:338
  181.5 1.3 collective-permute-start.23
  182.9 1.7 collective-permute-start.29
  185.5 3.1 %collective-permute-done.29 = bf16[216,128]{1,0:T(8,128)(2,1)S(1)} collective-permute-done((bf16[216,128]{1,0:T(8,128)(2,1)S(1)}, bf16[216,128]{1,0:T(8,128)(2,1)S(1)}, u32[]{:S(2)}, u32[]{:S(2)}) %collective-permute-start.29) | collective-permute-done | bytes 55328 | tf_op jit(solution)/shard_map/ppermute | solution.py:334
  188.6 1.4 collective-permute-start.30
  190.1 4.0 %collective-permute-done.30 = bf16[216,128]{1,0:T(8,128)(2,1)S(1)} collective-permute-done((bf16[216,128]{1,0:T(8,128)(2,1)S(1)}, bf16[216,128]{1,0:T(8,128)(2,1)S(1)}, u32[]{:S(2)}, u32[]{:S(2)}) %collective-permute-start.30) | collective-permute-done | bytes 55328 | tf_op jit(solution)/shard_map/ppermute | solution.py:338
  194.3 4.6 %collective-permute-done.31 = bf16[432,128]{1,0:T(8,128)(2,1)S(1)} collective-permute-done((bf16[432,128]{1,0:T(8,128)(2,1)S(1)}, bf16[432,128]{1,0:T(8,128)(2,1)S(1)}, u32[]{:S(2)}, u32[]{:S(2)}) %collective-permute-start.31) | collective-permute-done | bytes 110624 | tf_op jit(solution)/shard_map/ppermute | solution.py:338
  200.8 12.8 %backward_fine_0.1 = (f32[4,32,2048]{2,1,0:T(8,128)}, bf16[4,32,2048]{2,1,0:T(8,128)(2,1)}) custom-call(bf16[4,64,4096]{2,1,0:T(8,128)(2,1)} %grad_fine.1.grads, bf16[64,4096]{1,0:T(8,128)(2,1)} %copy-done.6, bf16[64,4096]{1,0:T(8,128)(2,1)} %copy-done.7, bf16[3,192,192]{2,1,0:T(8,128)(2,1)} %reshape.59.weights), custom_call_target="tpu_custom_call" | custom-call | tf_op jit(solution)/shard_map/backward_fine_0/pallas_call | solution.py:461
  213.6 1.5 collective-permute-start.16
  216.4 12.9 %backward_fine_1.1 = (f32[4,32,2048]{2,1,0:T(8,128)}, bf16[4,32,2048]{2,1,0:T(8,128)(2,1)}) custom-call(bf16[4,64,4096]{2,1,0:T(8,128)(2,1)} %grad_fine.1.grads, bf16[64,4096]{1,0:T(8,128)(2,1)} %copy-done.6, bf16[64,4096]{1,0:T(8,128)(2,1)} %copy-done.7, bf16[3,192,192]{2,1,0:T(8,128)(2,1)} %reshape.59.weights), custom_call_target="tpu_custom_call" | custom-call | tf_op jit(solution)/shard_map/backward_fine_1/pallas_call | solution.py:461
  230.2 9.5 %collective-permute-done.17 = bf16[4,32,2048]{2,1,0:T(8,128)(2,1)S(1)} collective-permute-done((bf16[4,32,2048]{2,1,0:T(8,128)(2,1)}, bf16[4,32,2048]{2,1,0:T(8,128)(2,1)S(1)}, u32[]{:S(2)}, u32[]{:S(2)}) %collective-permute-start.17) | collective-permute-done | bytes 524320 | tf_op jit(solution)/shard_map/ppermute | solution.py:320
  240.0 2.7 %copy.32 = f32[32,4,4096]{2,1,0:T(4,128)} copy(f32[32,4,4096]{2,0,1:T(8,128)S(1)} %maximum_bitcast_fusion) | data formatting | bytes 4194304
  242.8 1.3 convert_multiply_fusion
  (137 shorter events, 25.9 us)
Async XLA Ops:
  2.4 7.7 %copy-start.1 = (bf16[32,4,4096]{2,0,1:T(8,128)(2,1)}, bf16[32,4,4096]{2,0,1:T(8,128)(2,1)S(1)}, u32[]{:S(2)}) copy-start(bf16[32,4,4096]{2,0,1:T(8,128)(2,1)S(1)} %copy.35) | copy-start | bytes 3145732
  3.5 19.3 %copy-start.18 = (bf16[1728,64]{0,1:T(8,128)(2,1)S(1)}, bf16[1728,64]{0,1:T(8,128)(2,1)}, u32[]{:S(2)}) copy-start(bf16[1728,64]{0,1:T(8,128)(2,1)} %param.8) | copy-start | bytes 663556
  3.5 15.8 %collective-permute-start.2 = (bf16[2,32,4096]{2,1,0:T(8,128)(2,1)S(1)}, bf16[2,32,4096]{2,1,0:T(8,128)(2,1)S(1)}, u32[]{:S(2)}, u32[]{:S(2)}) collective-permute-start(bf16[2,32,4096]{2,1,0:T(8,128)(2,1)S(1)} %pad_maximum_fusion), channel_id=1, source_target_pairs={{0,1},{1,0},{2,3},{3,2},{4,5},{5,4},{6,7},{7,6},{8,9},{9,8},{10,11... | collective-permute-start | bytes 1572872 | tf_op jit(solution)/shard_map/ppermute | solution.py:320
  6.5 17.9 %collective-permute-start = (bf16[32,4096]{1,0:T(8,128)(2,1)}, bf16[32,4096]{1,0:T(8,128)(2,1)S(1)}, u32[]{:S(2)}, u32[]{:S(2)}) collective-permute-start(bf16[32,4096]{1,0:T(8,128)(2,1)} %get-tuple-element.35), channel_id=1, source_target_pairs={{0,2},{2,4},{4,6},{6,8},{8,10},{10,12},{12,14},{14,16},{16,18},{18... | collective-permute-start | bytes 786440 | tf_op jit(solution)/shard_map/ppermute | solution.py:311
  8.0 16.5 %collective-permute-start.1 = (bf16[32,4096]{1,0:T(8,128)(2,1)}, bf16[32,4096]{1,0:T(8,128)(2,1)S(1)}, u32[]{:S(2)}, u32[]{:S(2)}) collective-permute-start(bf16[32,4096]{1,0:T(8,128)(2,1)} %get-tuple-element.36), channel_id=1, source_target_pairs={{2,0},{4,2},{6,4},{8,6},{10,8},{12,10},{14,12},{16,14},{18,16},{20... | collective-permute-start | bytes 786440 | tf_op jit(solution)/shard_map/ppermute | solution.py:316
  10.1 19.6 %collective-permute-start.3 = (bf16[2,32,4096]{2,1,0:T(8,128)(2,1)}, bf16[2,32,4096]{2,1,0:T(8,128)(2,1)S(1)}, u32[]{:S(2)}, u32[]{:S(2)}) collective-permute-start(bf16[2,32,4096]{2,1,0:T(8,128)(2,1)} %slice.145), channel_id=1, source_target_pairs={{0,1},{1,0},{2,3},{3,2},{4,5},{5,4},{6,7},{7,6},{8,9},{9,8},{10,11... | collective-permute-start | bytes 1572872 | tf_op jit(solution)/shard_map/ppermute | solution.py:320
  19.3 5.2 %copy-start.3 = (bf16[2,32,4096]{2,1,0:T(8,128)(2,1)}, bf16[2,32,4096]{2,1,0:T(8,128)(2,1)S(1)}, u32[]{:S(2)}) copy-start(bf16[2,32,4096]{2,1,0:T(8,128)(2,1)S(1)} %collective-permute-done.2.edge) | copy-start | bytes 1572868
  20.2 9.5 %collective-permute-start.4 = (bf16[32,4096]{1,0:T(8,128)(2,1)}, bf16[32,4096]{1,0:T(8,128)(2,1)S(1)}, u32[]{:S(2)}, u32[]{:S(2)}) collective-permute-start(bf16[32,4096]{1,0:T(8,128)(2,1)} %get-tuple-element.43), channel_id=1, source_target_pairs={{0,2},{2,4},{4,6},{6,8},{8,10},{10,12},{12,14},{14,16},{16,18},{18... | collective-permute-start | bytes 786440 | tf_op jit(solution)/shard_map/ppermute | solution.py:311
  21.5 8.2 %collective-permute-start.5 = (bf16[32,4096]{1,0:T(8,128)(2,1)}, bf16[32,4096]{1,0:T(8,128)(2,1)S(1)}, u32[]{:S(2)}, u32[]{:S(2)}) collective-permute-start(bf16[32,4096]{1,0:T(8,128)(2,1)} %get-tuple-element.42), channel_id=1, source_target_pairs={{2,0},{4,2},{6,4},{8,6},{10,8},{12,10},{14,12},{16,14},{18,16},{20... | collective-permute-start | bytes 786440 | tf_op jit(solution)/shard_map/ppermute | solution.py:316
  24.5 5.2 %copy-start.8 = (bf16[32,4096]{1,0:T(8,128)(2,1)}, bf16[32,4096]{1,0:T(8,128)(2,1)S(1)}, u32[]{:S(2)}) copy-start(bf16[32,4096]{1,0:T(8,128)(2,1)S(1)} %collective-permute-done.low) | copy-start | bytes 786436
  24.5 5.2 %copy-start.9 = (bf16[32,4096]{1,0:T(8,128)(2,1)}, bf16[32,4096]{1,0:T(8,128)(2,1)S(1)}, u32[]{:S(2)}) copy-start(bf16[32,4096]{1,0:T(8,128)(2,1)S(1)} %collective-permute-done.1.high) | copy-start | bytes 786436
  29.7 0.9 copy-start.10
  29.7 1.0 copy-start.11
  59.8 15.5 %copy-start.4 = (bf16[3456,128]{1,0:T(8,128)(2,1)S(1)}, bf16[3456,128]{1,0:T(8,128)(2,1)}, u32[]{:S(2)}) copy-start(bf16[3456,128]{1,0:T(8,128)(2,1)} %param.9) | copy-start | bytes 2654212
  59.8 8.1 %collective-permute-start.8 = (bf16[2,64,1024]{2,1,0:T(8,128)(2,1)}, bf16[2,64,1024]{2,1,0:T(8,128)(2,1)S(1)}, u32[]{:S(2)}, u32[]{:S(2)}) collective-permute-start(bf16[2,64,1024]{2,1,0:T(8,128)(2,1)} %get-tuple-element.13.own), channel_id=1, source_target_pairs={{0,1},{1,0},{2,3},{3,2},{4,5},{5,4},{6,7},{7,6},{8,9},{9,8},{10,11... | collective-permute-start | bytes 786440 | tf_op jit(solution)/shard_map/ppermute | solution.py:320
  62.5 15.3 %collective-permute-start.6 = (bf16[64,1024]{1,0:T(8,128)(2,1)S(1)}, bf16[64,1024]{1,0:T(8,128)(2,1)S(1)}, u32[]{:S(2)}, u32[]{:S(2)}) collective-permute-start(bf16[64,1024]{1,0:T(8,128)(2,1)S(1)} %get-tuple-element.49), channel_id=1, source_target_pairs={{0,2},{2,4},{4,6},{6,8},{8,10},{10,12},{12,14},{14,16},{16,18},{18... | collective-permute-start | bytes 393224 | tf_op jit(solution)/shard_map/ppermute | solution.py:311
  66.1 11.7 %collective-permute-start.7 = (bf16[64,1024]{1,0:T(8,128)(2,1)S(1)}, bf16[64,1024]{1,0:T(8,128)(2,1)S(1)}, u32[]{:S(2)}, u32[]{:S(2)}) collective-permute-start(bf16[64,1024]{1,0:T(8,128)(2,1)S(1)} %get-tuple-element.48), channel_id=1, source_target_pairs={{2,0},{4,2},{6,4},{8,6},{10,8},{12,10},{14,12},{16,14},{18,16},{20... | collective-permute-start | bytes 393224 | tf_op jit(solution)/shard_map/ppermute | solution.py:316
  67.8 9.2 %copy-start.14 = (bf16[2,64,1024]{2,1,0:T(8,128)(2,1)}, bf16[2,64,1024]{2,1,0:T(8,128)(2,1)S(1)}, u32[]{:S(2)}) copy-start(bf16[2,64,1024]{2,1,0:T(8,128)(2,1)S(1)} %collective-permute-done.8.peer) | copy-start | bytes 786436
  68.6 9.3 %collective-permute-start.10 = (bf16[64,1024]{1,0:T(8,128)(2,1)}, bf16[64,1024]{1,0:T(8,128)(2,1)S(1)}, u32[]{:S(2)}, u32[]{:S(2)}) collective-permute-start(bf16[64,1024]{1,0:T(8,128)(2,1)} %get-tuple-element.46), channel_id=1, source_target_pairs={{2,0},{4,2},{6,4},{8,6},{10,8},{12,10},{14,12},{16,14},{18,16},{20... | collective-permute-start | bytes 393224 | tf_op jit(solution)/shard_map/ppermute | solution.py:316
  69.8 8.0 %collective-permute-start.9 = (bf16[64,1024]{1,0:T(8,128)(2,1)S(1)}, bf16[64,1024]{1,0:T(8,128)(2,1)S(1)}, u32[]{:S(2)}, u32[]{:S(2)}) collective-permute-start(bf16[64,1024]{1,0:T(8,128)(2,1)S(1)} %get-tuple-element.47), channel_id=1, source_target_pairs={{0,2},{2,4},{4,6},{6,8},{8,10},{10,12},{12,14},{14,16},{16,18},{18... | collective-permute-start | bytes 393224 | tf_op jit(solution)/shard_map/ppermute | solution.py:311
  86.0 14.5 %collective-permute-start.11 = (bf16[128,1024]{1,0:T(8,128)(2,1)S(1)}, bf16[128,1024]{1,0:T(8,128)(2,1)S(1)}, u32[]{:S(2)}, u32[]{:S(2)}) collective-permute-start(bf16[128,1024]{1,0:T(8,128)(2,1)S(1)} %get-tuple-element.41), channel_id=1, source_target_pairs={{0,2},{2,4},{4,6},{6,8},{8,10},{10,12},{12,14},{14,16},{16,18},{18... | collective-permute-start | bytes 786440 | tf_op jit(solution)/shard_map/ppermute | solution.py:311
  89.7 10.8 %collective-permute-start.12 = (bf16[128,1024]{1,0:T(8,128)(2,1)S(1)}, bf16[128,1024]{1,0:T(8,128)(2,1)S(1)}, u32[]{:S(2)}, u32[]{:S(2)}) collective-permute-start(bf16[128,1024]{1,0:T(8,128)(2,1)S(1)} %get-tuple-element.40), channel_id=1, source_target_pairs={{2,0},{4,2},{6,4},{8,6},{10,8},{12,10},{14,12},{16,14},{18,16},{20... | collective-permute-start | bytes 786440 | tf_op jit(solution)/shard_map/ppermute | solution.py:316
  100.5 8.5 %copy-start.2 = (bf16[3456,128]{1,0:T(8,128)(2,1)S(1)}, bf16[3456,128]{1,0:T(8,128)(2,1)}, u32[]{:S(2)}) copy-start(bf16[3456,128]{1,0:T(8,128)(2,1)} %kernel_grad_coarse.1) | copy-start | bytes 2654212
  107.2 8.6 %collective-permute-start.13 = (bf16[2,64,1024]{2,1,0:T(8,128)(2,1)}, bf16[2,64,1024]{2,1,0:T(8,128)(2,1)S(1)}, u32[]{:S(2)}, u32[]{:S(2)}) collective-permute-start(bf16[2,64,1024]{2,1,0:T(8,128)(2,1)} %get-tuple-element.16), channel_id=1, source_target_pairs={{0,1},{1,0},{2,3},{3,2},{4,5},{5,4},{6,7},{7,6},{8,9},{9,8},{10,11... | collective-permute-start | bytes 786440 | tf_op jit(solution)/shard_map/ppermute | solution.py:320
  109.0 41.2 %collective-permute-start.26 = (bf16[1728,128]{1,0:T(8,128)(2,1)S(1)}, bf16[1728,128]{1,0:T(8,128)(2,1)S(1)}, u32[]{:S(2)}, u32[]{:S(2)}) collective-permute-start(bf16[1728,128]{1,0:T(8,128)(2,1)S(1)} %broadcast_select_fusion.2), channel_id=1, source_target_pairs={{0,2},{2,0},{4,6},{6,4},{8,10},{10,8},{12,14},{14,12},{16,18},{18,... | collective-permute-start | bytes 1327112 | tf_op jit(solution)/shard_map/ppermute | solution.py:334
  149.5 9.8 %copy-start = (bf16[4,64,4096]{2,1,0:T(8,128)(2,1)S(1)}, bf16[4,64,4096]{2,1,0:T(8,128)(2,1)}, u32[]{:S(2)}) copy-start(bf16[4,64,4096]{2,1,0:T(8,128)(2,1)} %grad_fine.1.grads) | copy-start | bytes 6291460
  149.5 1.6 collective-permute-start.18
  151.2 6.4 %collective-permute-start.19 = (bf16[224,128]{1,0:T(8,128)(2,1)S(1)}, bf16[224,128]{1,0:T(8,128)(2,1)S(1)}, u32[]{:S(2)}, u32[]{:S(2)}) collective-permute-start(bf16[224,128]{1,0:T(8,128)(2,1)S(1)} %broadcast_select_fusion.14), channel_id=1, source_target_pairs={{0,4},{2,6},{4,0},{6,2},{8,12},{10,14},{12,8},{14,10},{16,20},{18,... | collective-permute-start | bytes 172040 | tf_op jit(solution)/shard_map/ppermute | solution.py:334
  155.4 13.8 %collective-permute-start.27 = (bf16[864,128]{1,0:T(8,128)(2,1)S(1)}, bf16[864,128]{1,0:T(8,128)(2,1)S(1)}, u32[]{:S(2)}, u32[]{:S(2)}) collective-permute-start(bf16[864,128]{1,0:T(8,128)(2,1)S(1)} %broadcast_select_fusion.5), channel_id=1, source_target_pairs={{0,4},{2,6},{4,0},{6,2},{8,12},{10,14},{12,8},{14,10},{16,20},{18,... | collective-permute-start | bytes 663560 | tf_op jit(solution)/shard_map/ppermute | solution.py:334
  157.7 4.4 %collective-permute-start.20 = (bf16[112,128]{1,0:T(8,128)(2,1)S(1)}, bf16[112,128]{1,0:T(8,128)(2,1)S(1)}, u32[]{:S(2)}, u32[]{:S(2)}) collective-permute-start(bf16[112,128]{1,0:T(8,128)(2,1)S(1)} %broadcast_select_fusion.20), channel_id=1, source_target_pairs={{0,8},{2,10},{4,12},{6,14},{8,0},{10,2},{12,4},{14,6},{16,24},{18,... | collective-permute-start | bytes 86024 | tf_op jit(solution)/shard_map/ppermute | solution.py:334
  159.4 39.7 %collective-permute-start.14 = (bf16[64,4096]{1,0:T(8,128)(2,1)S(1)}, bf16[64,4096]{1,0:T(8,128)(2,1)S(1)}, u32[]{:S(2)}, u32[]{:S(2)}) collective-permute-start(bf16[64,4096]{1,0:T(8,128)(2,1)S(1)} %get-tuple-element.33), channel_id=1, source_target_pairs={{0,2},{2,4},{4,6},{6,8},{8,10},{10,12},{12,14},{14,16},{16,18},{18... | collective-permute-start | bytes 1572872 | tf_op jit(solution)/shard_map/ppermute | solution.py:311
  160.7 38.4 %collective-permute-start.15 = (bf16[64,4096]{1,0:T(8,128)(2,1)S(1)}, bf16[64,4096]{1,0:T(8,128)(2,1)S(1)}, u32[]{:S(2)}, u32[]{:S(2)}) collective-permute-start(bf16[64,4096]{1,0:T(8,128)(2,1)S(1)} %get-tuple-element.32), channel_id=1, source_target_pairs={{2,0},{4,2},{6,4},{8,6},{10,8},{12,10},{14,12},{16,14},{18,16},{20... | collective-permute-start | bytes 1572872 | tf_op jit(solution)/shard_map/ppermute | solution.py:316
  162.1 14.6 %collective-permute-start.21 = (bf16[56,128]{1,0:T(8,128)(2,1)S(1)}, bf16[56,128]{1,0:T(8,128)(2,1)S(1)}, u32[]{:S(2)}, u32[]{:S(2)}) collective-permute-start(bf16[56,128]{1,0:T(8,128)(2,1)S(1)} %broadcast_select_fusion.23), channel_id=1, source_target_pairs={{0,16},{2,18},{4,20},{6,22},{8,24},{10,26},{12,28},{14,30},{16,0},... | collective-permute-start | bytes 43016 | tf_op jit(solution)/shard_map/ppermute | solution.py:334
  176.7 4.8 %collective-permute-start.22 = (bf16[56,128]{1,0:T(8,128)(2,1)S(1)}, bf16[56,128]{1,0:T(8,128)(2,1)S(1)}, u32[]{:S(2)}, u32[]{:S(2)}) collective-permute-start(bf16[56,128]{1,0:T(8,128)(2,1)S(1)} %add_convert_fusion.7), channel_id=1, source_target_pairs={{0,16},{2,18},{4,20},{6,22},{8,24},{10,26},{12,28},{14,30},{16,0},... | collective-permute-start | bytes 43016 | tf_op jit(solution)/shard_map/ppermute | solution.py:338
  176.8 6.0 %collective-permute-start.28 = (bf16[432,128]{1,0:T(8,128)(2,1)S(1)}, bf16[432,128]{1,0:T(8,128)(2,1)S(1)}, u32[]{:S(2)}, u32[]{:S(2)}) collective-permute-start(bf16[432,128]{1,0:T(8,128)(2,1)S(1)} %broadcast_select_fusion.11), channel_id=1, source_target_pairs={{0,8},{2,10},{4,12},{6,14},{8,0},{10,2},{12,4},{14,6},{16,24},{18,... | collective-permute-start | bytes 331784 | tf_op jit(solution)/shard_map/ppermute | solution.py:334
  181.5 3.9 %collective-permute-start.23 = (bf16[112,128]{1,0:T(8,128)(2,1)S(1)}, bf16[112,128]{1,0:T(8,128)(2,1)S(1)}, u32[]{:S(2)}, u32[]{:S(2)}) collective-permute-start(bf16[112,128]{1,0:T(8,128)(2,1)S(1)} %pad_maximum_fusion.7), channel_id=1, source_target_pairs={{0,8},{2,10},{4,12},{6,14},{8,0},{10,2},{12,4},{14,6},{16,24},{18,... | collective-permute-start | bytes 86024 | tf_op jit(solution)/shard_map/ppermute | solution.py:338
  182.9 5.7 %collective-permute-start.29 = (bf16[216,128]{1,0:T(8,128)(2,1)S(1)}, bf16[216,128]{1,0:T(8,128)(2,1)S(1)}, u32[]{:S(2)}, u32[]{:S(2)}) collective-permute-start(bf16[216,128]{1,0:T(8,128)(2,1)S(1)} %broadcast_select_fusion.17), channel_id=1, source_target_pairs={{0,16},{2,18},{4,20},{6,22},{8,24},{10,26},{12,28},{14,30},{16,0},... | collective-permute-start | bytes 165896 | tf_op jit(solution)/shard_map/ppermute | solution.py:334
  185.5 4.6 %collective-permute-start.24 = (bf16[224,128]{1,0:T(8,128)(2,1)S(1)}, bf16[224,128]{1,0:T(8,128)(2,1)S(1)}, u32[]{:S(2)}, u32[]{:S(2)}) collective-permute-start(bf16[224,128]{1,0:T(8,128)(2,1)S(1)} %pad_maximum_fusion.6), channel_id=1, source_target_pairs={{0,4},{2,6},{4,0},{6,2},{8,12},{10,14},{12,8},{14,10},{16,20},{18,... | collective-permute-start | bytes 172040 | tf_op jit(solution)/shard_map/ppermute | solution.py:338
  188.6 5.4 %collective-permute-start.30 = (bf16[216,128]{1,0:T(8,128)(2,1)S(1)}, bf16[216,128]{1,0:T(8,128)(2,1)S(1)}, u32[]{:S(2)}, u32[]{:S(2)}) collective-permute-start(bf16[216,128]{1,0:T(8,128)(2,1)S(1)} %add_convert_fusion.5), channel_id=1, source_target_pairs={{0,16},{2,18},{4,20},{6,22},{8,24},{10,26},{12,28},{14,30},{16,0},... | collective-permute-start | bytes 165896 | tf_op jit(solution)/shard_map/ppermute | solution.py:338
  194.1 4.8 %collective-permute-start.31 = (bf16[432,128]{1,0:T(8,128)(2,1)S(1)}, bf16[432,128]{1,0:T(8,128)(2,1)S(1)}, u32[]{:S(2)}, u32[]{:S(2)}) collective-permute-start(bf16[432,128]{1,0:T(8,128)(2,1)S(1)} %pad_maximum_fusion.5), channel_id=1, source_target_pairs={{0,8},{2,10},{4,12},{6,14},{8,0},{10,2},{12,4},{14,6},{16,24},{18,... | collective-permute-start | bytes 331784 | tf_op jit(solution)/shard_map/ppermute | solution.py:338
  194.2 4.9 %collective-permute-start.25 = (bf16[448,128]{1,0:T(8,128)(2,1)S(1)}, bf16[448,128]{1,0:T(8,128)(2,1)S(1)}, u32[]{:S(2)}, u32[]{:S(2)}) collective-permute-start(bf16[448,128]{1,0:T(8,128)(2,1)S(1)} %pad_maximum_fusion.4), channel_id=1, source_target_pairs={{0,2},{2,0},{4,6},{6,4},{8,10},{10,8},{12,14},{14,12},{16,18},{18,... | collective-permute-start | bytes 344072 | tf_op jit(solution)/shard_map/ppermute | solution.py:338
  199.0 30.8 %collective-permute-start.32 = (bf16[864,128]{1,0:T(8,128)(2,1)S(1)}, bf16[864,128]{1,0:T(8,128)(2,1)S(1)}, u32[]{:S(2)}, u32[]{:S(2)}) collective-permute-start(bf16[864,128]{1,0:T(8,128)(2,1)S(1)} %pad_maximum_fusion.3), channel_id=1, source_target_pairs={{0,4},{2,6},{4,0},{6,2},{8,12},{10,14},{12,8},{14,10},{16,20},{18,... | collective-permute-start | bytes 663560 | tf_op jit(solution)/shard_map/ppermute | solution.py:338
  199.2 0.8 copy-start.6
  213.6 16.5 %collective-permute-start.16 = (bf16[4,32,2048]{2,1,0:T(8,128)(2,1)}, bf16[4,32,2048]{2,1,0:T(8,128)(2,1)S(1)}, u32[]{:S(2)}, u32[]{:S(2)}) collective-permute-start(bf16[4,32,2048]{2,1,0:T(8,128)(2,1)} %get-tuple-element.19), channel_id=1, source_target_pairs={{0,1},{1,0},{2,3},{3,2},{4,5},{5,4},{6,7},{7,6},{8,9},{9,8},{10,11... | collective-permute-start | bytes 1572872 | tf_op jit(solution)/shard_map/ppermute | solution.py:320
  216.4 13.7 %copy-start.12 = (f32[4,32,2048]{2,1,0:T(8,128)S(1)}, f32[4,32,2048]{2,1,0:T(8,128)}, u32[]{:S(2)}) copy-start(f32[4,32,2048]{2,1,0:T(8,128)} %get-tuple-element.18) | copy-start | bytes 3145732
  229.3 10.4 %collective-permute-start.17 = (bf16[4,32,2048]{2,1,0:T(8,128)(2,1)}, bf16[4,32,2048]{2,1,0:T(8,128)(2,1)S(1)}, u32[]{:S(2)}, u32[]{:S(2)}) collective-permute-start(bf16[4,32,2048]{2,1,0:T(8,128)(2,1)} %get-tuple-element.21), channel_id=1, source_target_pairs={{0,1},{1,0},{2,3},{3,2},{4,5},{5,4},{6,7},{7,6},{8,9},{9,8},{10,11... | collective-permute-start | bytes 1572872 | tf_op jit(solution)/shard_map/ppermute | solution.py:320
  229.9 9.8 %copy-start.13 = (f32[4,32,2048]{2,1,0:T(8,128)S(1)}, f32[4,32,2048]{2,1,0:T(8,128)}, u32[]{:S(2)}) copy-start(f32[4,32,2048]{2,1,0:T(8,128)} %get-tuple-element.20) | copy-start | bytes 3145732
  230.0 12.7 %collective-permute-start.33 = (bf16[1728,128]{1,0:T(8,128)(2,1)S(1)}, bf16[1728,128]{1,0:T(8,128)(2,1)S(1)}, u32[]{:S(2)}, u32[]{:S(2)}) collective-permute-start(bf16[1728,128]{1,0:T(8,128)(2,1)S(1)} %pad_maximum_fusion.1), channel_id=1, source_target_pairs={{0,2},{2,0},{4,6},{6,4},{8,10},{10,8},{12,14},{14,12},{16,18},{18,... | collective-permute-start | bytes 1327112 | tf_op jit(solution)/shard_map/ppermute | solution.py:338
  (9 other events, 6.5 us)
